TPU v7x, 256 devices: a whole 4x4x8 slice. The times are simulated.
256 devices in a mesh: slot: 16 (over z, core), hid: 16 (over y, x).
Axes of the slice: x: 4, y: 4, z: 8, core: 2. Of those that a mesh axis runs over, the one named last changes fastest.
Arguments:
- cotangent: bfloat16 [32768, 2048], P('slot', 'hid'), may hold values from -6 to 6
- hidden: bfloat16 [32768, 8192], P('slot', 'hid'), may hold values from -6 to 6
- weights: bfloat16 [16, 8192, 2048], P('slot', 'hid'), may hold values from -0.125 to 0.125
- slot_experts: int32 [16, 1], replicated, may hold values from 0 to 3
- next_experts: int32 [16, 1], replicated, may hold values from 0 to 3
- row_counts: int32 [16], replicated, may hold values from 1 to 2048, 20480 in all
- master: float32 [4, 8192, 2048], P(None, 'hid', 'slot'), may hold values from -3 to 3
- momentum: float32 [4, 8192, 2048], P(None, 'hid', 'slot'), may hold values from -96 to 96
Outputs:
- input_grad: bfloat16 [32768, 8192], P('slot', 'hid')
- new_momentum: float32 [4, 8192, 2048], P(None, 'hid', 'slot')
- new_master: float32 [4, 8192, 2048], P(None, 'hid', 'slot')
- placed: bfloat16 [16, 8192, 2048], P('slot', 'hid')
Inputs may be any that keep to these rules, and one draw needn't show every extreme that they name: `slot_experts`: every expert 0 to 3 is held by at least one slot. `next_experts`: every expert 0 to 3 is held by at least one slot. `row_counts`: the counts sum to 20480.
All inputs are finite; a program needn't handle non-finite values.
Results may differ from a plain program's by a relative error of at most 0.015.
Values may be sent and summed in bfloat16 or wider, within the bound.
No kernel may reach another device: no remote copies, remote signals or barrier semaphores. Data moves between devices by JAX's collectives and lax.ppermute only.
A program may use at most 128 MiB of HBM per device.

v0:
```python
import jax
import jax.numpy as jnp
from jax import lax
from jax.sharding import PartitionSpec as P

momentum_decay = 0.9
learn_rate = 0.01


def local(cotangent, hidden, weights, slot_experts, next_experts, row_counts, master, momentum):
    row_span = hidden.shape[0]
    own_slot = lax.axis_index("slot")
    live_count = lax.dynamic_index_in_dim(row_counts, own_slot, 0, keepdims=False)
    live_mask = (jnp.arange(row_span, dtype=jnp.int32) < live_count)[:, None].astype(
        cotangent.dtype
    )
    masked = cotangent * live_mask
    weight_rows = weights[0]
    shard_piece = lax.all_gather(masked, "hid", axis=1, tiled=True)
    hid_grad = lax.dot_general(
        shard_piece, weight_rows, (((1,), (1,)), ((), ())), preferred_element_type=jnp.float32
    )
    w_part = lax.dot_general(
        hidden, shard_piece, (((0,), (0,)), ((), ())), preferred_element_type=jnp.float32
    )
    w_grad = w_part
    hid_grad, w_grad = (hid_grad, w_grad)
    input_grad = hid_grad.astype(jnp.bfloat16)
    expert_count = master.shape[0]
    owners = (
        slot_experts[:, 0][None, :] == jnp.arange(expert_count, dtype=jnp.int32)[:, None]
    ).astype(jnp.float32)
    own_weight = lax.dynamic_index_in_dim(owners, own_slot, 1, keepdims=False)
    stacked = own_weight[:, None, None] * w_grad[None]
    expert_grad = lax.psum_scatter(
        stacked.astype(jnp.bfloat16), "slot", scatter_dimension=2, tiled=True
    ).astype(jnp.float32)
    new_momentum = momentum_decay * momentum + expert_grad
    new_master = master - learn_rate * new_momentum
    rounded = new_master.astype(jnp.bfloat16)
    gathered = lax.all_gather(rounded, "slot", axis=2, tiled=True)
    target = lax.dynamic_index_in_dim(next_experts[:, 0], own_slot, 0, keepdims=False)
    placed = lax.dynamic_index_in_dim(gathered, target, 0, keepdims=True)
    return (input_grad, new_momentum, new_master, placed)


def solution(mesh):
    return jax.shard_map(
        local,
        mesh=mesh,
        in_specs=(
            P("slot", "hid"),
            P("slot", "hid"),
            P("slot", "hid", None),
            P(),
            P(),
            P(),
            P(None, "hid", "slot"),
            P(None, "hid", "slot"),
        ),
        out_specs=(
            P("slot", "hid"),
            P(None, "hid", "slot"),
            P(None, "hid", "slot"),
            P("slot", "hid", None),
        ),
        check_vma=False,
    )
```

profile of v0, /device:TPU:1, one launch (start us, length us, event | category | flops | bytes accessed | tf_op | source)
XLA Modules:
  0.0 297.3 jit_solution(14528464055429409936)
XLA Ops:
  7.2 0.0 all-gather.3.cloned.1.call-start
  7.2 1.4 dynamic_slice.15
  8.6 0.6 fusion.1
  9.3 2.2 broadcast_multiply_fusion
  11.4 0.0 all-gather.3.cloned.1.call-update
  11.5 0.0 reduce-scatter.4.cloned.1.call-start
  11.5 1.2 dynamic-slice.1
  12.8 0.6 fusion.2
  13.4 84.5 %all-gather.3.cloned.1.call-done = bf16[2048,2048]{1,0:T(8,128)(2,1)} async-done(((bf16[2048,128]{1,0:T(8,128)(2,1)}), bf16[2048,2048]{1,0:T(8,128)(2,1)}) %all-gather.3.cloned.1.call-update) | async-done | bytes 8388624 | tf_op jit(solution)/shard_map/all_gather | solution.py:19
  97.9 9.8 %convolution_bitcast_fusion = f32[512,2048]{0,1:T(8,128)} fusion(bf16[2048,2048]{1,0:T(8,128)(2,1)} %all-gather.3.cloned.1.call-done, bf16[2048,512]{1,0:T(8,128)(2,1)S(1)} %copy-done), kind=kOutput, calls=%fused_computation.1 | convolution fusion | flops 4294967296 | bytes 14680064 | tf_op jit(solution)/shard_map/dot_general | solution.py:23
  107.7 5.5 %copy.13 = f32[512,2048]{1,0:T(8,128)} copy(f32[512,2048]{0,1:T(8,128)} %convolution_bitcast_fusion) | data formatting | bytes 8388608 | tf_op jit(solution)/shard_map/dot_general | solution.py:23
  113.1 8.0 %multiply_convert_fusion = bf16[4,512,2048]{2,1,0:T(8,128)(2,1)} fusion(f32[512,2048]{1,0:T(8,128)} %copy.13, f32[4]{0:T(128)S(1)} %fusion.2), kind=kLoop, calls=%fused_computation | loop fusion | flops 8388608 | bytes 12582928 | tf_op jit(solution)/shard_map/convert_element_type | solution.py:36
  121.1 14.6 %copy.14 = bf16[4,512,2048]{1,0,2:T(4,128)(2,1)} copy(bf16[4,512,2048]{2,1,0:T(8,128)(2,1)} %multiply_convert_fusion) | data formatting | bytes 16777216
  135.7 10.2 %copy.16 = bf16[256,8,4,512]{3,1,2,0:T(8,128)(2,1)} copy(bf16[256,8,4,512]{3,2,1,0:T(4,128)(2,1)} %bitcast.18) | data formatting | bytes 16777216
  146.0 0.0 reduce-scatter.4.cloned.1.call-update
  146.0 0.2 all-gather.5.cloned.1.call-start
  146.2 68.0 %reduce-scatter.4.cloned.1.call-done = bf16[128,2048]{1,0:T(8,128)(2,1)} async-done(((bf16[2048,2048]{1,0:T(8,128)(2,1)}), bf16[128,2048]{1,0:T(8,128)(2,1)}) %reduce-scatter.4.cloned.1.call-update) | async-done | bytes 524304
  214.3 1.4 reshape.21
  215.7 0.4 copy.15
  216.1 3.2 %fusion.3 = (bf16[4,512,128]{2,1,0:T(8,128)(2,1)}, f32[4,512,128]{2,1,0:T(8,128)}, f32[4,512,128]{2,1,0:T(8,128)}) fusion(f32[4,512,128]{2,1,0:T(8,128)} %param.14, bf16[4,512,128]{2,1,0:T(8,128)(2,1)S(1)} %copy.15, f32[4,512,128]{2,1,0:T(8,128)} %param.15), kind=kLoop, calls=%fused_computation.13 | loop fusion | flops 1572864 | bytes 5242880 | tf_op jit(solution)/shard_map/convert_element_type | solution.py:40
  219.4 0.6 constant_dynamic-slice_fusion
  221.9 9.9 %convolution_convert_fusion = bf16[2048,512]{1,0:T(8,128)(2,1)} fusion(bf16[2048,2048]{1,0:T(8,128)(2,1)} %all-gather.3.cloned.1.call-done, bf16[1,512,2048]{2,1,0:T(8,128)(2,1)} %param.10), kind=kOutput, calls=%fused_computation.2 | convolution fusion | flops 4296015872 | bytes 12582912 | tf_op jit(solution)/shard_map/dot_general | solution.py:20
  231.8 55.9 %all-gather.5.cloned.1.call-done = bf16[4,512,2048]{2,1,0:T(8,128)(2,1)} async-done(((bf16[4,512,128]{2,1,0:T(8,128)(2,1)}), bf16[4,512,2048]{2,1,0:T(8,128)(2,1)}) %all-gather.5.cloned.1.call-update) | async-done | bytes 8388624 | tf_op jit(solution)/shard_map/all_gather | solution.py:41
  287.6 3.2 %constant_dynamic-slice_fusion.1 = bf16[1,512,2048]{2,1,0:T(8,128)(2,1)} fusion(bf16[4,512,2048]{2,1,0:T(8,128)(2,1)} %all-gather.5.cloned.1.call-done, s32[]{:T(128)S(6)} %select_n.12), kind=kLoop, calls=%fused_computation.12 | loop fusion | bytes 4194308 | tf_op jit(solution)/shard_map/jit(dynamic_index_in_dim)/dynamic_slice | solution.py:43
  (5 shorter events, 0.0 us)
Async XLA Ops:
  7.2 90.8 %copy-start = (bf16[2048,512]{1,0:T(8,128)(2,1)S(1)}, bf16[2048,512]{1,0:T(8,128)(2,1)}, u32[]{:S(2)}) copy-start(bf16[2048,512]{1,0:T(8,128)(2,1)} %param.9) | copy-start | bytes 6291460
  7.2 90.7 %all-gather.3.cloned.1.call-start = ((), (), s32[]{:S(2)}) async-start(), calls=%async_computation.1 | async-start | bytes 8912896 | tf_op jit(solution)/shard_map/all_gather | solution.py:19
  11.5 202.8 %reduce-scatter.4.cloned.1.call-start = ((), (), s32[]{:S(2)}) async-start(), calls=%async_computation.3 | async-start | bytes 8912896
  146.0 73.4 %copy-start.1 = (s32[16,1]{0,1:T(1,128)S(1)}, s32[16,1]{0,1:T(1,128)}, u32[]{:S(2)}) copy-start(s32[16,1]{0,1:T(1,128)} %param.12) | copy-start | bytes 196
  146.0 141.6 %all-gather.5.cloned.1.call-start = ((), (), s32[]{:S(2)}) async-start(), calls=%async_computation.2 | async-start | bytes 8912896 | tf_op jit(solution)/shard_map/all_gather | solution.py:41
Sparse Core Ops, SparseCore 0:
  11.6 86.2 all-gather.2
  146.1 68.1 reduce-scatter.3
  219.5 68.0 all-gather.4
where the time goes:
time: 298 us; the launch traced here: 297 us
  waiting for transfers between devices  208 us (70%)
  local copies, waits for them, and re-layouts  38.5 us (13%)
  matrix products  19.6 us (7%)
  between operations  15.7 us (5%)
  other arithmetic  14.7 us (5%)
    all_gather x1, waiting for transfers between devices, local(): shard_piece = lax.all_gather(masked, 'hid', axis=1, tiled=True)  84.5 us
    unnamed x4, waiting for transfers between devices  68.1 us
    all_gather x1, waiting for transfers between devices, local(): gathered = lax.all_gather(rounded, 'slot', axis=2, tiled=True)  55.9 us
    unnamed x8, local copies, waits for them, and re-layouts  26.7 us
    dot_general x1, matrix products, local(): lax.dot_general(shard_piece, weight_rows, (((1,), (1,)), ((), ())), prefe...  9.86 us
    dot_general x1, matrix products, local(): lax.dot_general(hidden, shard_piece, (((0,), (0,)), ((), ())), preferred_...  9.75 us
    convert_element_type x1, other arithmetic, local(): stacked.astype(jnp.bfloat16)  8 us
  transfers between devices with their start and end apart: 3, of which 3 were waited for; matrix products, arithmetic and copies ran while one was open for 4% of the time, Pallas kernels for 0%

commit v1 on v0

--- a/solution.py
+++ b/solution.py
@@ -5,6 +5,32 @@
 
 momentum_decay = 0.9
 learn_rate = 0.01
+
+
+def recast_the_steps_all(patch, join_dim):
+    d_next = list(patch.shape[1:])
+    d_next[join_dim] *= patch.shape[0]
+    return jnp.moveaxis(patch, 0, join_dim).reshape(d_next)
+
+
+def _do_block(z_in, comm_axis, array_axis):
+    amount_of = lax.axis_size(comm_axis)
+    history = [(dd, (dd + 1) % amount_of) for dd in range(amount_of)]
+    then, main = ([], [])
+    panels = [(m, hop_no) for hop_no, m in history]
+    for rr in range(amount_of - 1):
+        if rr % 2 == 0:
+            r2 = lax.ppermute(then[-1] if then else z_in, comm_axis, history)
+            then.append(r2)
+        else:
+            z1 = lax.ppermute(main[-1] if main else z_in, comm_axis, panels)
+            main.append(z1)
+    field_out = jnp.stack([*then[::-1], z_in, *main])
+    opened = lax.axis_index(comm_axis)
+    local_now = len(then)
+    ready = opened - local_now
+    field_out = field_out[(jnp.arange(amount_of) - ready) % amount_of]
+    return recast_the_steps_all(field_out, array_axis)
 
 
 def local(cotangent, hidden, weights, slot_experts, next_experts, row_counts, master, momentum):
@@ -16,7 +42,7 @@
     )
     masked = cotangent * live_mask
     weight_rows = weights[0]
-    shard_piece = lax.all_gather(masked, "hid", axis=1, tiled=True)
+    shard_piece = _do_block(masked, "hid", 1)
     hid_grad = lax.dot_general(
         shard_piece, weight_rows, (((1,), (1,)), ((), ())), preferred_element_type=jnp.float32
     )

time: 298 us -> 367 us (1.23)
  local copies, waits for them, and re-layouts: 38.5 us -> 82.6 us
  starting transfers between devices: 0.3 us -> 37.4 us
  waiting for transfers between devices: 208 us -> 196 us
    all_gather x1 -> x0, waiting for transfers between devices: 84.5 us -> none  [local(): shard_piece = lax.all_gather(masked, 'hid', axis=1, tiled=True)]
    ppermute x0 -> x15, waiting for transfers between devices: none -> 63.4 us  [the longest x8 63.1 us: _do_block(): r2 = lax.ppermute(then[-1] if then else z_in, comm_axis, history)]
    ppermute x0 -> x15, starting transfers between devices: none -> 37.1 us  [the longest x7 35 us: _do_block(): z1 = lax.ppermute(main[-1] if main else z_in, comm_axis, panels)]
    unnamed x8 -> x56, local copies, waits for them, and re-layouts: 26.7 us -> 49.4 us
    transpose x0 -> x1, local copies, waits for them, and re-layouts: none -> 12.4 us  [recast_the_steps_all(): return jnp.moveaxis(patch, 0, join_dim).reshape(d_next)]
    unnamed x4 -> x3, waiting for transfers between devices: 68.1 us -> 77.2 us
    gather x0 -> x1, local copies, waits for them, and re-layouts: none -> 8.17 us  [_do_block(): field_out = field_out[(jnp.arange(amount_of) - ready) % amount_of]]
  transfers between devices with their start and end apart: 3 -> 17, of which waited for: 3 -> 11; matrix products, arithmetic and copies ran while one was open for 4% -> 10% of each run, Pallas kernels for 0% -> 0%
where the time goes in v1:
time: 367 us; the launch traced here: 366 us
  waiting for transfers between devices  196 us (53%)
  local copies, waits for them, and re-layouts  82.6 us (23%)
  starting transfers between devices  37.4 us (10%)
  matrix products  19.5 us (5%)
  between operations  16.2 us (4%)
  other arithmetic  13.6 us (4%)
    unnamed x3, waiting for transfers between devices  77.2 us
    ppermute x8, waiting for transfers between devices, _do_block(): r2 = lax.ppermute(then[-1] if then else z_in, comm_axis, history)  63.1 us
    all_gather x1, waiting for transfers between devices, local(): gathered = lax.all_gather(rounded, 'slot', axis=2, tiled=True)  55.9 us
    unnamed x56, local copies, waits for them, and re-layouts  49.4 us
    ppermute x7, starting transfers between devices, _do_block(): z1 = lax.ppermute(main[-1] if main else z_in, comm_axis, panels)  35 us
    transpose x1, local copies, waits for them, and re-layouts, recast_the_steps_all(): return jnp.moveaxis(patch, 0, join_dim).reshape(d_next)  12.4 us
    dot_general x1, matrix products, local(): lax.dot_general(shard_piece, weight_rows, (((1,), (1,)), ((), ())), prefe...  10 us
    dot_general x1, matrix products, local(): lax.dot_general(hidden, shard_piece, (((0,), (0,)), ((), ())), preferred_...  9.46 us
  transfers between devices with their start and end apart: 17, of which 11 were waited for; matrix products, arithmetic and copies ran while one was open for 10% of the time, Pallas kernels for 0%

profile of v1, /device:TPU:1, one launch (start us, length us, event | category | flops | bytes accessed | tf_op | source)
XLA Modules:
  0.0 365.8 jit_solution(16002875004977719110)
XLA Ops:
  12.8 13.4 %collective-permute-done = bf16[2048,128]{1,0:T(8,128)(2,1)S(1)} collective-permute-done((bf16[2048,128]{1,0:T(8,128)(2,1)S(1)}, bf16[2048,128]{1,0:T(8,128)(2,1)S(1)}, u32[]{:S(2)}, u32[]{:S(2)}) %collective-permute-start) | collective-permute-done | bytes 524320 | tf_op jit(solution)/shard_map/ppermute | solution.py:23
  26.2 4.8 %collective-permute-start.8 = (bf16[2048,128]{1,0:T(8,128)(2,1)S(1)}, bf16[2048,128]{1,0:T(8,128)(2,1)S(1)}, u32[]{:S(2)}, u32[]{:S(2)}) collective-permute-start(bf16[2048,128]{1,0:T(8,128)(2,1)S(1)} %broadcast_multiply_fusion), channel_id=1, source_target_pairs={{1,0},{2,1},{3,2},{4,3},{5,4},{6,5},{7,6},{8,7},{9,8},{10,9},{11,1... | collective-permute-start | bytes 1572872 | tf_op jit(solution)/shard_map/ppermute | solution.py:26
  31.0 8.8 %collective-permute-done.1 = bf16[2048,128]{1,0:T(8,128)(2,1)S(1)} collective-permute-done((bf16[2048,128]{1,0:T(8,128)(2,1)S(1)}, bf16[2048,128]{1,0:T(8,128)(2,1)S(1)}, u32[]{:S(2)}, u32[]{:S(2)}) %collective-permute-start.1) | collective-permute-done | bytes 524320 | tf_op jit(solution)/shard_map/ppermute | solution.py:23
  45.4 7.1 %collective-permute-done.2 = bf16[2048,128]{1,0:T(8,128)(2,1)S(1)} collective-permute-done((bf16[2048,128]{1,0:T(8,128)(2,1)S(1)}, bf16[2048,128]{1,0:T(8,128)(2,1)S(1)}, u32[]{:S(2)}, u32[]{:S(2)}) %collective-permute-start.2) | collective-permute-done | bytes 524320 | tf_op jit(solution)/shard_map/ppermute | solution.py:23
  52.5 5.3 %collective-permute-start.10 = (bf16[2048,128]{1,0:T(8,128)(2,1)S(1)}, bf16[2048,128]{1,0:T(8,128)(2,1)S(1)}, u32[]{:S(2)}, u32[]{:S(2)}) collective-permute-start(bf16[2048,128]{1,0:T(8,128)(2,1)S(1)} %collective-permute-done.9), channel_id=1, source_target_pairs={{1,0},{2,1},{3,2},{4,3},{5,4},{6,5},{7,6},{8,7},{9,8},{10,9},{11,1... | collective-permute-start | bytes 1572872 | tf_op jit(solution)/shard_map/ppermute | solution.py:26
  57.7 6.4 %collective-permute-done.3 = bf16[2048,128]{1,0:T(8,128)(2,1)S(1)} collective-permute-done((bf16[2048,128]{1,0:T(8,128)(2,1)S(1)}, bf16[2048,128]{1,0:T(8,128)(2,1)S(1)}, u32[]{:S(2)}, u32[]{:S(2)}) %collective-permute-start.3) | collective-permute-done | bytes 524320 | tf_op jit(solution)/shard_map/ppermute | solution.py:23
  64.2 4.9 %collective-permute-start.11 = (bf16[2048,128]{1,0:T(8,128)(2,1)S(1)}, bf16[2048,128]{1,0:T(8,128)(2,1)S(1)}, u32[]{:S(2)}, u32[]{:S(2)}) collective-permute-start(bf16[2048,128]{1,0:T(8,128)(2,1)S(1)} %collective-permute-done.10), channel_id=1, source_target_pairs={{1,0},{2,1},{3,2},{4,3},{5,4},{6,5},{7,6},{8,7},{9,8},{10,9},{11,1... | collective-permute-start | bytes 1572872 | tf_op jit(solution)/shard_map/ppermute | solution.py:26
  69.1 6.4 %collective-permute-done.4 = bf16[2048,128]{1,0:T(8,128)(2,1)S(1)} collective-permute-done((bf16[2048,128]{1,0:T(8,128)(2,1)S(1)}, bf16[2048,128]{1,0:T(8,128)(2,1)S(1)}, u32[]{:S(2)}, u32[]{:S(2)}) %collective-permute-start.4) | collective-permute-done | bytes 524320 | tf_op jit(solution)/shard_map/ppermute | solution.py:23
  76.3 4.9 %collective-permute-start.12 = (bf16[2048,128]{1,0:T(8,128)(2,1)S(1)}, bf16[2048,128]{1,0:T(8,128)(2,1)}, u32[]{:S(2)}, u32[]{:S(2)}) collective-permute-start(bf16[2048,128]{1,0:T(8,128)(2,1)S(1)} %collective-permute-done.11), channel_id=1, source_target_pairs={{1,0},{2,1},{3,2},{4,3},{5,4},{6,5},{7,6},{8,7},{9,8},{10,9},{11,1... | collective-permute-start | bytes 1572872 | tf_op jit(solution)/shard_map/ppermute | solution.py:26
  81.2 6.3 %collective-permute-done.5 = bf16[2048,128]{1,0:T(8,128)(2,1)S(1)} collective-permute-done((bf16[2048,128]{1,0:T(8,128)(2,1)S(1)}, bf16[2048,128]{1,0:T(8,128)(2,1)S(1)}, u32[]{:S(2)}, u32[]{:S(2)}) %collective-permute-start.5) | collective-permute-done | bytes 524320 | tf_op jit(solution)/shard_map/ppermute | solution.py:23
  87.7 5.3 %collective-permute-start.13 = (bf16[2048,128]{1,0:T(8,128)(2,1)}, bf16[2048,128]{1,0:T(8,128)(2,1)}, u32[]{:S(2)}, u32[]{:S(2)}) collective-permute-start(bf16[2048,128]{1,0:T(8,128)(2,1)} %collective-permute-done.12), channel_id=1, source_target_pairs={{1,0},{2,1},{3,2},{4,3},{5,4},{6,5},{7,6},{8,7},{9,8},{10,9},{11,1... | collective-permute-start | bytes 1572872 | tf_op jit(solution)/shard_map/ppermute | solution.py:26
  93.1 7.7 %collective-permute-done.6 = bf16[2048,128]{1,0:T(8,128)(2,1)} collective-permute-done((bf16[2048,128]{1,0:T(8,128)(2,1)S(1)}, bf16[2048,128]{1,0:T(8,128)(2,1)}, u32[]{:S(2)}, u32[]{:S(2)}) %collective-permute-start.6) | collective-permute-done | bytes 524320 | tf_op jit(solution)/shard_map/ppermute | solution.py:23
  102.7 5.0 %collective-permute-start.14 = (bf16[2048,128]{1,0:T(8,128)(2,1)}, bf16[2048,128]{1,0:T(8,128)(2,1)S(1)}, u32[]{:S(2)}, u32[]{:S(2)}) collective-permute-start(bf16[2048,128]{1,0:T(8,128)(2,1)} %collective-permute-done.13), channel_id=1, source_target_pairs={{1,0},{2,1},{3,2},{4,3},{5,4},{6,5},{7,6},{8,7},{9,8},{10,9},{11,1... | collective-permute-start | bytes 1572872 | tf_op jit(solution)/shard_map/ppermute | solution.py:26
  107.8 7.1 %collective-permute-done.7 = bf16[2048,128]{1,0:T(8,128)(2,1)} collective-permute-done((bf16[2048,128]{1,0:T(8,128)(2,1)}, bf16[2048,128]{1,0:T(8,128)(2,1)}, u32[]{:S(2)}, u32[]{:S(2)}) %collective-permute-start.7) | collective-permute-done | bytes 524320 | tf_op jit(solution)/shard_map/ppermute | solution.py:23
  138.1 8.2 %gather_fusion = bf16[16,2048,128]{2,1,0:T(8,128)(2,1)} fusion(bf16[16,2048,128]{2,1,0:T(8,128)(2,1)} %bitcast_dynamic-update-slice_fusion, s32[1024]{0:T(1024)S(1)} %pad_clamp_fusion), kind=kCustom, calls=%fused_computation | custom fusion | bytes 16777280 | tf_op jit(solution)/shard_map/gather | solution.py:32
  146.2 12.4 %copy.16 = bf16[2048,16,128]{0,2,1:T(8,128)(2,1)} copy(bf16[2048,16,128]{2,0,1:T(8,128)(2,1)} %bitcast.53) | data formatting | bytes 16777216 | tf_op jit(solution)/shard_map/transpose | solution.py:13
  158.6 9.5 %convolution_bitcast_fusion = f32[512,2048]{0,1:T(8,128)} fusion(bf16[2048,2048]{0,1:T(8,128)(2,1)} %bitcast.56, bf16[2048,512]{1,0:T(8,128)(2,1)S(1)} %copy-done), kind=kOutput, calls=%fused_computation.2 | convolution fusion | flops 4294967296 | bytes 14680064 | tf_op jit(solution)/shard_map/dot_general | solution.py:49
  168.1 5.4 %copy.17 = f32[512,2048]{1,0:T(8,128)} copy(f32[512,2048]{0,1:T(8,128)} %convolution_bitcast_fusion) | data formatting | bytes 8388608 | tf_op jit(solution)/shard_map/dot_general | solution.py:49
  173.4 8.0 %multiply_convert_fusion = bf16[4,512,2048]{2,1,0:T(8,128)(2,1)} fusion(f32[512,2048]{1,0:T(8,128)} %copy.17, f32[4]{0:T(128)S(1)} %fusion.2), kind=kLoop, calls=%fused_computation.1 | loop fusion | flops 8388608 | bytes 12582928 | tf_op jit(solution)/shard_map/convert_element_type | solution.py:62
  181.5 14.5 %copy.18 = bf16[4,512,2048]{1,0,2:T(4,128)(2,1)} copy(bf16[4,512,2048]{2,1,0:T(8,128)(2,1)} %multiply_convert_fusion) | data formatting | bytes 16777216
  196.0 10.3 %copy.20 = bf16[256,8,4,512]{3,1,2,0:T(8,128)(2,1)} copy(bf16[256,8,4,512]{3,2,1,0:T(4,128)(2,1)} %bitcast.55) | data formatting | bytes 16777216
  206.6 77.1 %reduce-scatter.4.cloned.1.call-done = bf16[128,2048]{1,0:T(8,128)(2,1)} async-done(((bf16[2048,2048]{1,0:T(8,128)(2,1)}), bf16[128,2048]{1,0:T(8,128)(2,1)}) %reduce-scatter.4.cloned.1.call-update) | async-done | bytes 524304
  289.8 10.0 %convolution_convert_fusion = bf16[2048,512]{1,0:T(8,128)(2,1)} fusion(bf16[2048,2048]{0,1:T(8,128)(2,1)} %bitcast.57, bf16[1,512,2048]{2,1,0:T(8,128)(2,1)} %param.10), kind=kOutput, calls=%fused_computation.3 | convolution fusion | flops 4296015872 | bytes 12582912 | tf_op jit(solution)/shard_map/dot_general | solution.py:46
  299.9 55.9 %all-gather.2.cloned.1.call-done = bf16[4,512,2048]{2,1,0:T(8,128)(2,1)} async-done(((bf16[4,512,128]{2,1,0:T(8,128)(2,1)}), bf16[4,512,2048]{2,1,0:T(8,128)(2,1)}) %all-gather.2.cloned.1.call-update) | async-done | bytes 8388624 | tf_op jit(solution)/shard_map/all_gather | solution.py:67
  (86 shorter events, 44.9 us)
Async XLA Ops:
  7.2 151.4 %copy-start = (bf16[2048,512]{1,0:T(8,128)(2,1)S(1)}, bf16[2048,512]{1,0:T(8,128)(2,1)}, u32[]{:S(2)}) copy-start(bf16[2048,512]{1,0:T(8,128)(2,1)} %param.9) | copy-start | bytes 6291460
  7.2 121.7 %copy-start.2 = (bf16[2048,128]{1,0:T(8,128)(2,1)S(1)}, bf16[2048,128]{1,0:T(8,128)(2,1)}, u32[]{:S(2)}) copy-start(bf16[2048,128]{1,0:T(8,128)(2,1)} %param.8) | copy-start | bytes 1572868
  7.2 276.5 %reduce-scatter.4.cloned.1.call-start = ((), (), s32[]{:S(2)}) async-start(), calls=%async_computation.2 | async-start | bytes 8912896
  10.7 15.5 %collective-permute-start = (bf16[2048,128]{1,0:T(8,128)(2,1)S(1)}, bf16[2048,128]{1,0:T(8,128)(2,1)S(1)}, u32[]{:S(2)}, u32[]{:S(2)}) collective-permute-start(bf16[2048,128]{1,0:T(8,128)(2,1)S(1)} %broadcast_multiply_fusion), channel_id=1, source_target_pairs={{0,1},{1,2},{2,3},{3,4},{4,5},{5,6},{6,7},{7,8},{8,9},{9,10},{10,1... | collective-permute-start | bytes 1572872 | tf_op jit(solution)/shard_map/ppermute | solution.py:23
  26.2 13.6 %collective-permute-start.1 = (bf16[2048,128]{1,0:T(8,128)(2,1)S(1)}, bf16[2048,128]{1,0:T(8,128)(2,1)S(1)}, u32[]{:S(2)}, u32[]{:S(2)}) collective-permute-start(bf16[2048,128]{1,0:T(8,128)(2,1)S(1)} %collective-permute-done), channel_id=1, source_target_pairs={{0,1},{1,2},{2,3},{3,4},{4,5},{5,6},{6,7},{7,8},{8,9},{9,10},{10,1... | collective-permute-start | bytes 1572872 | tf_op jit(solution)/shard_map/ppermute | solution.py:23
  26.2 13.6 %collective-permute-start.8 = (bf16[2048,128]{1,0:T(8,128)(2,1)S(1)}, bf16[2048,128]{1,0:T(8,128)(2,1)S(1)}, u32[]{:S(2)}, u32[]{:S(2)}) collective-permute-start(bf16[2048,128]{1,0:T(8,128)(2,1)S(1)} %broadcast_multiply_fusion), channel_id=1, source_target_pairs={{1,0},{2,1},{3,2},{4,3},{5,4},{6,5},{7,6},{8,7},{9,8},{10,9},{11,1... | collective-permute-start | bytes 1572872 | tf_op jit(solution)/shard_map/ppermute | solution.py:26
  39.8 12.6 %collective-permute-start.2 = (bf16[2048,128]{1,0:T(8,128)(2,1)S(1)}, bf16[2048,128]{1,0:T(8,128)(2,1)S(1)}, u32[]{:S(2)}, u32[]{:S(2)}) collective-permute-start(bf16[2048,128]{1,0:T(8,128)(2,1)S(1)} %collective-permute-done.1), channel_id=1, source_target_pairs={{0,1},{1,2},{2,3},{3,4},{4,5},{5,6},{6,7},{7,8},{8,9},{9,10},{10,1... | collective-permute-start | bytes 1572872 | tf_op jit(solution)/shard_map/ppermute | solution.py:23
  40.6 11.8 %collective-permute-start.9 = (bf16[2048,128]{1,0:T(8,128)(2,1)S(1)}, bf16[2048,128]{1,0:T(8,128)(2,1)S(1)}, u32[]{:S(2)}, u32[]{:S(2)}) collective-permute-start(bf16[2048,128]{1,0:T(8,128)(2,1)S(1)} %collective-permute-done.8), channel_id=1, source_target_pairs={{1,0},{2,1},{3,2},{4,3},{5,4},{6,5},{7,6},{8,7},{9,8},{10,9},{11,1... | collective-permute-start | bytes 1572872 | tf_op jit(solution)/shard_map/ppermute | solution.py:26
  52.4 11.7 %collective-permute-start.3 = (bf16[2048,128]{1,0:T(8,128)(2,1)S(1)}, bf16[2048,128]{1,0:T(8,128)(2,1)S(1)}, u32[]{:S(2)}, u32[]{:S(2)}) collective-permute-start(bf16[2048,128]{1,0:T(8,128)(2,1)S(1)} %collective-permute-done.2), channel_id=1, source_target_pairs={{0,1},{1,2},{2,3},{3,4},{4,5},{5,6},{6,7},{7,8},{8,9},{9,10},{10,1... | collective-permute-start | bytes 1572872 | tf_op jit(solution)/shard_map/ppermute | solution.py:23
  52.5 11.7 %collective-permute-start.10 = (bf16[2048,128]{1,0:T(8,128)(2,1)S(1)}, bf16[2048,128]{1,0:T(8,128)(2,1)S(1)}, u32[]{:S(2)}, u32[]{:S(2)}) collective-permute-start(bf16[2048,128]{1,0:T(8,128)(2,1)S(1)} %collective-permute-done.9), channel_id=1, source_target_pairs={{1,0},{2,1},{3,2},{4,3},{5,4},{6,5},{7,6},{8,7},{9,8},{10,9},{11,1... | collective-permute-start | bytes 1572872 | tf_op jit(solution)/shard_map/ppermute | solution.py:26
  64.1 11.4 %collective-permute-start.4 = (bf16[2048,128]{1,0:T(8,128)(2,1)S(1)}, bf16[2048,128]{1,0:T(8,128)(2,1)S(1)}, u32[]{:S(2)}, u32[]{:S(2)}) collective-permute-start(bf16[2048,128]{1,0:T(8,128)(2,1)S(1)} %collective-permute-done.3), channel_id=1, source_target_pairs={{0,1},{1,2},{2,3},{3,4},{4,5},{5,6},{6,7},{7,8},{8,9},{9,10},{10,1... | collective-permute-start | bytes 1572872 | tf_op jit(solution)/shard_map/ppermute | solution.py:23
  64.2 11.3 %collective-permute-start.11 = (bf16[2048,128]{1,0:T(8,128)(2,1)S(1)}, bf16[2048,128]{1,0:T(8,128)(2,1)S(1)}, u32[]{:S(2)}, u32[]{:S(2)}) collective-permute-start(bf16[2048,128]{1,0:T(8,128)(2,1)S(1)} %collective-permute-done.10), channel_id=1, source_target_pairs={{1,0},{2,1},{3,2},{4,3},{5,4},{6,5},{7,6},{8,7},{9,8},{10,9},{11,1... | collective-permute-start | bytes 1572872 | tf_op jit(solution)/shard_map/ppermute | solution.py:26
  75.5 12.0 %collective-permute-start.5 = (bf16[2048,128]{1,0:T(8,128)(2,1)S(1)}, bf16[2048,128]{1,0:T(8,128)(2,1)S(1)}, u32[]{:S(2)}, u32[]{:S(2)}) collective-permute-start(bf16[2048,128]{1,0:T(8,128)(2,1)S(1)} %collective-permute-done.4), channel_id=1, source_target_pairs={{0,1},{1,2},{2,3},{3,4},{4,5},{5,6},{6,7},{7,8},{8,9},{9,10},{10,1... | collective-permute-start | bytes 1572872 | tf_op jit(solution)/shard_map/ppermute | solution.py:23
  76.3 11.4 %collective-permute-start.12 = (bf16[2048,128]{1,0:T(8,128)(2,1)S(1)}, bf16[2048,128]{1,0:T(8,128)(2,1)}, u32[]{:S(2)}, u32[]{:S(2)}) collective-permute-start(bf16[2048,128]{1,0:T(8,128)(2,1)S(1)} %collective-permute-done.11), channel_id=1, source_target_pairs={{1,0},{2,1},{3,2},{4,3},{5,4},{6,5},{7,6},{8,7},{9,8},{10,9},{11,1... | collective-permute-start | bytes 1572872 | tf_op jit(solution)/shard_map/ppermute | solution.py:26
  87.5 13.2 %collective-permute-start.6 = (bf16[2048,128]{1,0:T(8,128)(2,1)S(1)}, bf16[2048,128]{1,0:T(8,128)(2,1)}, u32[]{:S(2)}, u32[]{:S(2)}) collective-permute-start(bf16[2048,128]{1,0:T(8,128)(2,1)S(1)} %collective-permute-done.5), channel_id=1, source_target_pairs={{0,1},{1,2},{2,3},{3,4},{4,5},{5,6},{6,7},{7,8},{8,9},{9,10},{10,1... | collective-permute-start | bytes 1572872 | tf_op jit(solution)/shard_map/ppermute | solution.py:23
  87.7 15.0 %collective-permute-start.13 = (bf16[2048,128]{1,0:T(8,128)(2,1)}, bf16[2048,128]{1,0:T(8,128)(2,1)}, u32[]{:S(2)}, u32[]{:S(2)}) collective-permute-start(bf16[2048,128]{1,0:T(8,128)(2,1)} %collective-permute-done.12), channel_id=1, source_target_pairs={{1,0},{2,1},{3,2},{4,3},{5,4},{6,5},{7,6},{8,7},{9,8},{10,9},{11,1... | collective-permute-start | bytes 1572872 | tf_op jit(solution)/shard_map/ppermute | solution.py:26
  100.7 14.2 %collective-permute-start.7 = (bf16[2048,128]{1,0:T(8,128)(2,1)}, bf16[2048,128]{1,0:T(8,128)(2,1)}, u32[]{:S(2)}, u32[]{:S(2)}) collective-permute-start(bf16[2048,128]{1,0:T(8,128)(2,1)} %collective-permute-done.6), channel_id=1, source_target_pairs={{0,1},{1,2},{2,3},{3,4},{4,5},{5,6},{6,7},{7,8},{8,9},{9,10},{10,1... | collective-permute-start | bytes 1572872 | tf_op jit(solution)/shard_map/ppermute | solution.py:23
  102.0 30.6 %copy-start.14 = (bf16[2048,128]{1,0:T(8,128)(2,1)S(1)}, bf16[2048,128]{1,0:T(8,128)(2,1)}, u32[]{:S(2)}) copy-start(bf16[2048,128]{1,0:T(8,128)(2,1)} %copy-done.13) | copy-start | bytes 1572868
  102.7 34.4 %collective-permute-start.14 = (bf16[2048,128]{1,0:T(8,128)(2,1)}, bf16[2048,128]{1,0:T(8,128)(2,1)S(1)}, u32[]{:S(2)}, u32[]{:S(2)}) collective-permute-start(bf16[2048,128]{1,0:T(8,128)(2,1)} %collective-permute-done.13), channel_id=1, source_target_pairs={{1,0},{2,1},{3,2},{4,3},{5,4},{6,5},{7,6},{8,7},{9,8},{10,9},{11,1... | collective-permute-start | bytes 1572872 | tf_op jit(solution)/shard_map/ppermute | solution.py:26
  206.3 79.3 %copy-start.3 = (f32[4,512,128]{2,1,0:T(8,128)S(1)}, f32[4,512,128]{2,1,0:T(8,128)}, u32[]{:S(2)}) copy-start(f32[4,512,128]{2,1,0:T(8,128)} %param.14) | copy-start | bytes 3145732
  206.3 79.3 %copy-start.4 = (f32[4,512,128]{2,1,0:T(8,128)S(1)}, f32[4,512,128]{2,1,0:T(8,128)}, u32[]{:S(2)}) copy-start(f32[4,512,128]{2,1,0:T(8,128)} %param.15) | copy-start | bytes 3145732
  206.3 81.0 %copy-start.18 = (s32[16,1]{0,1:T(1,128)S(1)}, s32[16,1]{0,1:T(1,128)}, u32[]{:S(2)}) copy-start(s32[16,1]{0,1:T(1,128)} %param.12) | copy-start | bytes 196
  206.3 149.5 %all-gather.2.cloned.1.call-start = ((), (), s32[]{:S(2)}) async-start(), calls=%async_computation.1 | async-start | bytes 8912896 | tf_op jit(solution)/shard_map/all_gather | solution.py:67
  289.8 69.1 %copy-start.1 = (bf16[2048,512]{1,0:T(8,128)(2,1)S(1)}, bf16[2048,512]{1,0:T(8,128)(2,1)}, u32[]{:S(2)}) copy-start(bf16[2048,512]{1,0:T(8,128)(2,1)} %param.9) | copy-start | bytes 6291460
  (12 other events, 177.3 us)
Sparse Core Ops, SparseCore 0:
  206.4 77.2 reduce-scatter.3
  287.4 68.2 all-gather.1
